TPU v7x, 32 devices: a whole 2x2x4 slice. The times are simulated.
32 devices in a mesh: parts: 2 (over y), blk: 4 (over z), fsdp: 2 (over x), dp: 2 (over core).
Axes of the slice: x: 2, y: 2, z: 4, core: 2. Of those that a mesh axis runs over, the one named last changes fastest.
Arguments:
- tokens: bfloat16 [3072, 2304], P(('parts', 'blk', 'dp'), 'fsdp'), parts along dimension 0, may hold values from -6 to 6
- targets: bfloat16 [3072, 4, 2304], P(('parts', 'blk', 'dp'), None, 'fsdp'), parts along dimension 0, may hold values from -6 to 6
- enc_weight: bfloat16 [2304, 16384], P('fsdp', 'blk'), may hold values from -0.125 to 0.125
- enc_bias: float32 [16384], P('blk'), may hold values from -3 to 3
- dec_weight: bfloat16 [4, 16384, 2304], P(None, 'blk', 'fsdp'), may hold values from -0.046875 to 0.046875
- active_blocks: int32 [24, 32], P('parts'), parts along dimension 0, may hold values from 0 to 127, as said below
Outputs:
- enc_grad: bfloat16 [4608, 16384], P(('parts', 'fsdp', 'dp'), 'blk'), parts along dimension 0
- dec_grad: bfloat16 [8, 16384, 2304], P('parts', 'blk', ('fsdp', 'dp')), parts along dimension 0
There are 2 independent parts, one for each index of `parts`. A program takes and returns all parts, laid end to end along the dimension named above; an argument that names none is the same for every part. Nothing has to cross between parts.
Inputs may be any that keep to these rules, and one draw needn't show every extreme that they name: `active_blocks`: each row lists 32 different latent blocks; every latent block is listed by some row.
All inputs are finite; a program needn't handle non-finite values.
Results may differ from a plain program's by a relative error of at most 0.022.
Values may be sent and summed in bfloat16 or wider, within the bound.
A program may use at most 320 MiB of HBM per device.

v0:
```python
import jax
import jax.numpy as jnp
from jax import lax
from jax.sharding import PartitionSpec as P

LATBLK = 128
TOKBLK = 128


def swapped(block, axis, bit):
    count = lax.axis_size(axis)
    route = []
    for low in range(count):
        high = low | 1 << bit
        if high != low and high < count:
            route += [(low, high), (high, low)]
    return lax.ppermute(block, axis, route)


def on_device(tokens, targets, enc_weight, enc_bias, dec_weight, active_blocks):
    tok_rows = tokens.shape[0]
    panel_width = tokens.shape[1]
    latent_cols = enc_weight.shape[1]
    data_count = lax.axis_size("dp")
    shard_index = lax.axis_index("blk")
    pair_index = lax.axis_index("dp")
    token_blocks = active_blocks.shape[0]
    grad_scale = 2.0 / token_blocks
    group_tokens = lax.all_gather(tokens, "blk", axis=0, tiled=True)
    group_rows = group_tokens.shape[0]
    positions = jnp.arange(group_rows, dtype=jnp.int32)
    source_dev = positions // tok_rows
    global_row = (source_dev * data_count + pair_index) * tok_rows + positions % tok_rows
    row_block = global_row // TOKBLK
    row_onehot = (row_block[:, None] == jnp.arange(token_blocks, dtype=jnp.int32)[None, :]).astype(
        jnp.float32
    )
    partial_value = jnp.dot(group_tokens, enc_weight, preferred_element_type=jnp.float32)
    pre_total = lax.psum(partial_value.astype(jnp.bfloat16), "fsdp").astype(jnp.float32)
    positive = jnp.maximum(pre_total + enc_bias, 0.0)
    col_block = (shard_index * latent_cols + jnp.arange(latent_cols, dtype=jnp.int32)) // LATBLK
    present = jnp.any(active_blocks[:, :, None] == col_block[None, None, :], axis=1).astype(
        jnp.float32
    )
    latent_on = jnp.dot(row_onehot, present, preferred_element_type=jnp.float32)
    latent_on, positive, activations = (
        latent_on,
        positive,
        (latent_on * positive * positive).astype(jnp.bfloat16),
    )
    rebuilt = lax.psum_scatter(
        jnp.einsum(
            "tf,kfj->tkj", activations, dec_weight, preferred_element_type=jnp.float32
        ).astype(jnp.bfloat16),
        "blk",
        scatter_dimension=0,
        tiled=True,
    ).astype(jnp.float32)
    own_grad = (grad_scale * (rebuilt - targets.astype(jnp.float32))).astype(jnp.bfloat16)
    residual_grad = lax.all_gather(own_grad, "blk", axis=0, tiled=True)
    back_part = jnp.einsum(
        "tkj,kfj->tf", residual_grad, dec_weight, preferred_element_type=jnp.float32
    )
    act_grad = lax.psum(back_part.astype(jnp.bfloat16), "fsdp").astype(jnp.float32)
    pre_grad = (act_grad * latent_on * 2.0 * positive).astype(jnp.bfloat16)
    enc_term = jnp.einsum(
        "ti,tf->if", group_tokens, pre_grad, preferred_element_type=jnp.float32
    ).astype(jnp.bfloat16)
    dec_term = jnp.einsum(
        "tf,tkj->kfj", activations, residual_grad, preferred_element_type=jnp.float32
    ).astype(jnp.bfloat16)
    half_rows = panel_width // 2
    keep_start = pair_index * half_rows
    send_start = (1 - pair_index) * half_rows
    keep_enc = lax.dynamic_slice_in_dim(enc_term, keep_start, half_rows, 0)
    send_enc = lax.dynamic_slice_in_dim(enc_term, send_start, half_rows, 0)
    keep_dec = lax.dynamic_slice_in_dim(dec_term, keep_start, half_rows, 2)
    send_dec = lax.dynamic_slice_in_dim(dec_term, send_start, half_rows, 2)
    got_enc, got_dec = swapped((send_enc, send_dec), "dp", 0)
    enc_grad = (keep_enc.astype(jnp.float32) + got_enc.astype(jnp.float32)).astype(jnp.bfloat16)
    dec_grad = (keep_dec.astype(jnp.float32) + got_dec.astype(jnp.float32)).astype(jnp.bfloat16)
    return (enc_grad, dec_grad)


def solution(mesh):
    return jax.shard_map(
        on_device,
        mesh=mesh,
        in_specs=(
            P(("parts", "blk", "dp"), "fsdp"),
            P(("parts", "blk", "dp"), None, "fsdp"),
            P("fsdp", "blk"),
            P("blk"),
            P(None, "blk", "fsdp"),
            P("parts", None),
        ),
        out_specs=(P(("parts", "fsdp", "dp"), "blk"), P("parts", "blk", ("fsdp", "dp"))),
        check_vma=False,
    )
```

profile of v0, /device:TPU:24, one launch (start us, length us, event | category | flops | bytes accessed | tf_op | source)
XLA Modules:
  0.0 825.1 jit_solution(12597523745914928915)
XLA Ops:
  7.2 0.0 all-gather.3.cloned.1.call-start
  7.2 0.7 all-gather.3.cloned.1.call-update
  7.9 0.0 all-reduce.3.cloned.1.call-start
  8.0 41.0 %all-gather.3.cloned.1.call-done = bf16[768,1152]{1,0:T(8,128)(2,1)} async-done(((bf16[192,1152]{1,0:T(8,128)(2,1)}), bf16[768,1152]{1,0:T(8,128)(2,1)}) %all-gather.3.cloned.1.call-update) | async-done | bytes 1769488 | tf_op jit(solution)/shard_map/all_gather | solution.py:29
  49.0 13.0 %convolution_convert_fusion.3 = bf16[768,4096]{1,0:T(8,128)(2,1)} fusion(bf16[768,1152]{1,0:T(8,128)(2,1)} %all-gather.3.cloned.1.call-done, bf16[1152,4096]{1,0:T(8,128)(2,1)} %param.8), kind=kOutput, calls=%fused_computation.13 | convolution fusion | flops 7250903040 | bytes 17498112 | tf_op jit(solution)/shard_map/dot_general | solution.py:38
  62.0 0.0 all-reduce.3.cloned.1.call-update
  62.1 0.0 copy-start.2
  62.1 0.0 reduce-scatter.2.cloned.1.call-start
  62.2 1.4 compare_reduce_fusion
  63.6 7.0 fusion.7
  70.7 145.5 %all-reduce.3.cloned.1.call-done = bf16[768,4096]{1,0:T(8,128)(2,1)} async-done(((bf16[768,4096]{1,0:T(8,128)(2,1)}), bf16[768,4096]{1,0:T(8,128)(2,1)}) %all-reduce.3.cloned.1.call-update) | async-done | bytes 6291472 | tf_op jit(solution)/shard_map/psum | solution.py:39
  216.2 7.6 fusion.3
  223.8 2.6 copy-done
  226.4 34.4 %convolution_convert_fusion.2 = bf16[768,4,1152]{2,0,1:T(8,128)(2,1)} fusion(bf16[768,4096,1]{1,0,2:T(8,128)(2,1)S(1)} %fusion.3, bf16[4,4096,1152]{2,1,0:T(8,128)(2,1)} %param.10), kind=kOutput, calls=%fused_computation.12 | convolution fusion | flops 28994568192 | bytes 51118080 | tf_op jit(solution)/shard_map/tf,kfj->tkj/dot_general | solution.py:52
  260.8 0.0 reduce-scatter.2.cloned.1.call-update
  260.8 0.0 all-gather.5.cloned.1.call-start
  260.9 122.9 %reduce-scatter.2.cloned.1.call-done = bf16[192,4,1152]{2,0,1:T(8,128)(2,1)} async-done(((bf16[768,4,1152]{2,0,1:T(8,128)(2,1)}), bf16[192,4,1152]{2,0,1:T(8,128)(2,1)}) %reduce-scatter.2.cloned.1.call-update) | async-done | bytes 1769488 | tf_op jit(solution)/shard_map/reduce_scatter | solution.py:51
  383.7 3.2 multiply_convert_fusion.2
  386.9 0.0 all-gather.5.cloned.1.call-update
  387.0 0.2 all-reduce.5.cloned.1.call-start
  387.2 126.4 %all-gather.5.cloned.1.call-done = bf16[768,4,1152]{2,0,1:T(8,128)(2,1)} async-done(((bf16[192,4,1152]{2,0,1:T(8,128)(2,1)}), bf16[768,4,1152]{2,0,1:T(8,128)(2,1)}) %all-gather.5.cloned.1.call-update) | async-done | bytes 7077904 | tf_op jit(solution)/shard_map/all_gather | solution.py:60
  513.6 37.4 %convolution_convert_fusion = bf16[4,1152,4096]{2,1,0:T(8,128)(2,1)} fusion(bf16[768,4,1152]{2,0,1:T(8,128)(2,1)} %all-gather.5.cloned.1.call-done, bf16[768,4096,1]{1,0,2:T(8,128)(2,1)} %copy-done), kind=kOutput, calls=%fused_computation | convolution fusion | flops 29009903616 | bytes 51118080 | tf_op jit(solution)/shard_map/tf,tkj->kfj/dot_general | solution.py:69
  551.0 16.8 %dynamic-slice_bitcast_fusion = bf16[4,4096,576]{1,2,0:T(8,128)(2,1)} fusion(bf16[4,1152,4096]{2,1,0:T(8,128)(2,1)} %convolution_convert_fusion, s32[]{:T(128)S(6)} %select_n.49), kind=kLoop, calls=%fused_computation.4 | loop fusion | bytes 37748740 | tf_op jit(solution)/shard_map/dynamic_slice | solution.py:78
  567.7 0.0 collective-permute-start.1
  567.8 37.0 %bitcast_convert_fusion = bf16[768,4096]{1,0:T(8,128)(2,1)} fusion(bf16[768,4,1152]{2,0,1:T(8,128)(2,1)} %all-gather.5.cloned.1.call-done, bf16[4,4096,1152]{2,1,0:T(8,128)(2,1)} %param.10), kind=kOutput, calls=%fused_computation.7 | convolution fusion | flops 28994174976 | bytes 51118080 | tf_op jit(solution)/shard_map/tkj,kfj->tf/dot_general | solution.py:61
  604.7 0.0 all-reduce.5.cloned.1.call-update
  604.8 154.6 %all-reduce.5.cloned.1.call-done = bf16[768,4096]{1,0:T(8,128)(2,1)} async-done(((bf16[768,4096]{1,0:T(8,128)(2,1)}), bf16[768,4096]{1,0:T(8,128)(2,1)}) %all-reduce.5.cloned.1.call-update) | async-done | bytes 6291472 | tf_op jit(solution)/shard_map/psum | solution.py:64
  759.4 15.0 %convolution_convert_fusion.1 = bf16[4096,1152]{0,1:T(8,128)(2,1)} fusion(bf16[768,1152]{1,0:T(8,128)(2,1)S(1)} %copy-done.5, f32[768,4096]{1,0:T(8,128)} %fusion.7, bf16[768,4096]{1,0:T(8,128)(2,1)} %all-reduce.5.cloned.1.call-done, bf16[768,4096]{1,0:T(8,128)(2,1)} %all-reduce.3.cloned.1.call-done, f32[4096]{0:T(1024)S(1)} %copy-done.3), kind=kOutput, calls=%fused_computation.5 | convolution fusion | flops 7277641728 | bytes 36388864 | tf_op jit(solution)/shard_map/ti,tf->if/dot_general | solution.py:66
  774.4 5.1 dynamic-slice_bitcast_fusion.1
  779.5 8.2 collective-permute-done
  787.7 8.0 fusion.2
  795.8 22.8 %fusion = bf16[4,4096,576]{1,2,0:T(8,128)(2,1)} fusion(bf16[4,4096,576]{1,2,0:T(8,128)(2,1)} %collective-permute-done.1, bf16[4,1152,4096]{2,1,0:T(8,128)(2,1)} %convolution_convert_fusion, s32[]{:T(128)S(6)} %select_n.48), kind=kLoop, calls=%fused_computation.2 | loop fusion | flops 37748736 | bytes 56623108 | tf_op jit(solution)/shard_map/convert_element_type | solution.py:81
  (14 shorter events, 0.1 us)
Async XLA Ops:
  7.2 41.8 %all-gather.3.cloned.1.call-start = ((), (), s32[]{:S(2)}) async-start(), calls=%async_computation.1 | async-start | bytes 2211840 | tf_op jit(solution)/shard_map/all_gather | solution.py:29
  7.9 54.3 %copy-start.4 = (s32[12,32]{1,0:T(8,128)S(1)}, s32[12,32]{1,0:T(8,128)}, u32[]{:S(2)}) copy-start(s32[12,32]{1,0:T(8,128)} %param.11) | copy-start | bytes 4612
  7.9 208.3 %all-reduce.3.cloned.1.call-start = ((), (), s32[]{:S(2)}) async-start(), calls=%async_computation.2 | async-start | bytes 12582912 | tf_op jit(solution)/shard_map/psum | solution.py:39
  62.1 154.1 %copy-start.2 = (f32[4096]{0:T(1024)S(1)}, f32[4096]{0:T(1024)}, u32[]{:S(2)}) copy-start(f32[4096]{0:T(1024)} %param.9) | copy-start | bytes 49156
  62.1 321.6 %reduce-scatter.2.cloned.1.call-start = ((), (), s32[]{:S(2)}) async-start(), calls=%async_computation.3 | async-start | bytes 8847360 | tf_op jit(solution)/shard_map/reduce_scatter | solution.py:51
  223.8 2.6 copy-start
  226.4 157.3 %copy-start.1 = (bf16[192,4,1152]{2,1,0:T(4,128)(2,1)S(1)}, bf16[192,4,1152]{2,1,0:T(4,128)(2,1)}, u32[]{:S(2)}) copy-start(bf16[192,4,1152]{2,1,0:T(4,128)(2,1)} %param.7) | copy-start | bytes 5308420
  260.8 252.7 %all-gather.5.cloned.1.call-start = ((), (), s32[]{:S(2)}) async-start(), calls=%async_computation.4 | async-start | bytes 8847360 | tf_op jit(solution)/shard_map/all_gather | solution.py:60
  387.0 372.4 %all-reduce.5.cloned.1.call-start = ((), (), s32[]{:S(2)}) async-start(), calls=%async_computation.5 | async-start | bytes 12582912 | tf_op jit(solution)/shard_map/psum | solution.py:64
  567.7 191.6 %copy-start.3 = (f32[4096]{0:T(1024)S(1)}, f32[4096]{0:T(1024)}, u32[]{:S(2)}) copy-start(f32[4096]{0:T(1024)} %param.9) | copy-start | bytes 49156
  567.7 191.6 %copy-start.5 = (bf16[768,1152]{1,0:T(8,128)(2,1)S(1)}, bf16[768,1152]{1,0:T(8,128)(2,1)}, u32[]{:S(2)}) copy-start(bf16[768,1152]{1,0:T(8,128)(2,1)} %all-gather.3.cloned.1.call-done) | copy-start | bytes 5308420
  567.7 228.0 %collective-permute-start.1 = (bf16[4,4096,576]{1,2,0:T(8,128)(2,1)}, bf16[4,4096,576]{1,2,0:T(8,128)(2,1)}, u32[]{:S(2)}, u32[]{:S(2)}) collective-permute-start(bf16[4,4096,576]{1,2,0:T(8,128)(2,1)} %dynamic-slice_bitcast_fusion), channel_id=1, source_target_pairs={{0,1},{1,0},{2,3},{3,2},{4,5},{5,4},{6,7},{7,6},{8,9},{9,8},{10,11... | collective-permute-start | bytes 56623112 | tf_op jit(solution)/shard_map/ppermute | solution.py:17
  779.5 8.3 %collective-permute-start = (bf16[576,4096]{1,0:T(8,128)(2,1)}, bf16[576,4096]{1,0:T(8,128)(2,1)}, u32[]{:S(2)}, u32[]{:S(2)}) collective-permute-start(bf16[576,4096]{1,0:T(8,128)(2,1)} %dynamic-slice_bitcast_fusion.1), channel_id=1, source_target_pairs={{0,1},{1,0},{2,3},{3,2},{4,5},{5,4},{6,7},{7,6},{8,9},{9,8},{10,11... | collective-permute-start | bytes 14155784 | tf_op jit(solution)/shard_map/ppermute | solution.py:17
Sparse Core Ops, SparseCore 0:
  9.6 39.3 all-gather.2
  62.2 153.9 all-reduce.2
  260.9 122.7 reduce-scatter.1
  387.1 126.4 all-gather.4
  604.9 154.4 all-reduce.4
where the time goes:
time: 827 us; the launch traced here: 825 us
  waiting for transfers between devices  599 us (72%)
  matrix products  144 us (17%)
  other arithmetic  43.1 us (5%)
  local copies, waits for them, and re-layouts  24.5 us (3%)
  between operations  13.9 us (2%)
    psum x1, waiting for transfers between devices, on_device(): lax.psum(back_part.astype(jnp.bfloat16), 'fsdp').astype(jnp.float32)  155 us
    psum x1, waiting for transfers between devices, on_device(): lax.psum(partial_value.astype(jnp.bfloat16), 'fsdp').astype(jnp.float32)  146 us
    all_gather x1, waiting for transfers between devices, on_device(): residual_grad = lax.all_gather(own_grad, 'blk', axis=0, tiled=True)  126 us
    reduce_scatter x1, waiting for transfers between devices, on_device(): lax.psum_scatter(jnp.einsum('tf,kfj->tkj', activations, dec_weight, prefe...  123 us
    all_gather x1, waiting for transfers between devices, on_device(): group_tokens = lax.all_gather(tokens, 'blk', axis=0, tiled=True)  41 us
    dot_general x1, matrix products, on_device(): jnp.einsum('tf,tkj->kfj', activations, residual_grad, preferred_element_t...  37.4 us
    dot_general x1, matrix products, on_device(): jnp.einsum('tkj,kfj->tf', residual_grad, dec_weight, preferred_element_ty...  37 us
    dot_general x1, matrix products, on_device(): jnp.einsum('tf,kfj->tkj', activations, dec_weight, preferred_element_type...  34.4 us
  transfers between devices with their start and end apart: 7, of which 6 were waited for; matrix products, arithmetic and copies ran while one was open for 9% of the time, Pallas kernels for 0%

commit v1 on v0

v1 whole, which is shorter than its diff:
```python
import functools

import jax
import jax.numpy as jnp
import numpy as np
from jax import lax
from jax.experimental import pallas as pl
from jax.experimental.pallas import tpu as pltpu
from jax.sharding import PartitionSpec as P

LATBLK = 128
TOKBLK = 128
F32 = jnp.float32
BF16 = jnp.bfloat16
VMEM_LIMIT = 32 * 1024 * 1024


def swapped(block, axis, bit):
    count = lax.axis_size(axis)
    route = []
    for low in range(count):
        high = low | 1 << bit
        if high != low and high < count:
            route += [(low, high), (high, low)]
    return lax.ppermute(block, axis, route)


def dense_tail(
    group_tokens, targets, enc_weight, enc_bias, dec_weight, active_blocks
):
    tok_rows = targets.shape[0]
    latent_cols = enc_weight.shape[1]
    data_count = lax.axis_size("dp")
    shard_index = lax.axis_index("blk")
    pair_index = lax.axis_index("dp")
    token_blocks = active_blocks.shape[0]
    grad_scale = 2.0 / token_blocks
    group_rows = group_tokens.shape[0]
    positions = jnp.arange(group_rows, dtype=jnp.int32)
    source_dev = positions // tok_rows
    global_row = (source_dev * data_count + pair_index) * tok_rows + positions % tok_rows
    row_block = global_row // TOKBLK
    row_onehot = (row_block[:, None] == jnp.arange(token_blocks, dtype=jnp.int32)[None, :]).astype(F32)
    partial_value = jnp.dot(group_tokens, enc_weight, preferred_element_type=F32)
    pre_total = lax.psum(partial_value.astype(BF16), "fsdp").astype(F32)
    positive = jnp.maximum(pre_total + enc_bias, 0.0)
    col_block = (shard_index * latent_cols + jnp.arange(latent_cols, dtype=jnp.int32)) // LATBLK
    present = jnp.any(active_blocks[:, :, None] == col_block[None, None, :], axis=1).astype(F32)
    latent_on = jnp.dot(row_onehot, present, preferred_element_type=F32)
    activations = (latent_on * positive * positive).astype(BF16)
    rebuilt = lax.psum_scatter(
        jnp.einsum("tf,kfj->tkj", activations, dec_weight, preferred_element_type=F32).astype(BF16),
        "blk",
        scatter_dimension=0,
        tiled=True,
    ).astype(F32)
    own_grad = (grad_scale * (rebuilt - targets.astype(F32))).astype(BF16)
    residual_grad = lax.all_gather(own_grad, "blk", axis=0, tiled=True)
    back_part = jnp.einsum("tkj,kfj->tf", residual_grad, dec_weight, preferred_element_type=F32)
    act_grad = lax.psum(back_part.astype(BF16), "fsdp").astype(F32)
    pre_grad = (act_grad * latent_on * 2.0 * positive).astype(BF16)
    return weight_grads(group_tokens, pre_grad, activations, residual_grad)


def weight_grads(group_tokens, pre_grad, activations, residual_grad):
    pair_index = lax.axis_index("dp")
    half = group_tokens.shape[1] // 2
    keep_start = pair_index * half
    send_start = (1 - pair_index) * half

    def dec_of(start):
        part = lax.dynamic_slice_in_dim(residual_grad, start, half, 2)
        return jnp.einsum("tf,tkj->kfj", activations, part, preferred_element_type=F32).astype(BF16)

    def enc_of(start):
        part = lax.dynamic_slice_in_dim(group_tokens, start, half, 1)
        return jnp.einsum("ti,tf->if", part, pre_grad, preferred_element_type=F32).astype(BF16)

    got_dec = swapped(dec_of(send_start), "dp", 0)
    keep_dec = dec_of(keep_start)
    got_enc = swapped(enc_of(send_start), "dp", 0)
    keep_enc = enc_of(keep_start)
    enc_grad = (keep_enc.astype(F32) + got_enc.astype(F32)).astype(BF16)
    dec_grad = (keep_dec.astype(F32) + got_dec.astype(F32)).astype(BF16)
    return (enc_grad, dec_grad)


def tile_at(code, lat_blocks, unit):
    row = pl.multiple_of((code // lat_blocks) * unit, unit)
    col = pl.multiple_of((code % lat_blocks) * LATBLK, LATBLK)
    return pl.ds(row, unit), pl.ds(col, LATBLK)


def pack_kernel(lat_blocks, unit, code_ref, dense_ref, packed_ref):
    @pl.loop(0, packed_ref.shape[0])
    def _(slot):
        rows, cols = tile_at(code_ref[slot], lat_blocks, unit)
        packed_ref[slot] = dense_ref[rows, cols]


def act_kernel(lat_blocks, unit, code_ref, mine_ref, other_ref, bias_ref, act_ref):
    act_ref[...] = jnp.zeros_like(act_ref)

    @pl.loop(0, code_ref[mine_ref.shape[0]])
    def _(slot):
        rows, cols = tile_at(code_ref[slot], lat_blocks, unit)
        pre = mine_ref[slot].astype(F32) + other_ref[slot].astype(F32) + bias_ref[:, cols]
        positive = jnp.maximum(pre, 0.0)
        act_ref[rows, cols] = (positive * positive).astype(BF16)


def pre_grad_kernel(
    lat_blocks, unit, code_ref, mine_ref, other_ref, bias_ref, back_mine_ref, back_other_ref, out_ref
):
    out_ref[...] = jnp.zeros_like(out_ref)

    @pl.loop(0, code_ref[mine_ref.shape[0]])
    def _(slot):
        rows, cols = tile_at(code_ref[slot], lat_blocks, unit)
        pre = mine_ref[slot].astype(F32) + other_ref[slot].astype(F32) + bias_ref[:, cols]
        grad = back_mine_ref[slot].astype(F32) + back_other_ref[slot].astype(F32)
        out_ref[rows, cols] = (grad * (2.0 * jnp.maximum(pre, 0.0))).astype(BF16)


def on_tiles(kernel, out_shape, codes, *arrays):
    size = out_shape.size * 2 + sum(array.size * array.dtype.itemsize for array in arrays)
    return pl.pallas_call(
        kernel,
        out_shape=out_shape,
        in_specs=[pl.BlockSpec(memory_space=pltpu.SMEM)]
        + [pl.BlockSpec(memory_space=pltpu.VMEM)] * len(arrays),
        out_specs=pl.BlockSpec(memory_space=pltpu.VMEM),
        compiler_params=pltpu.CompilerParams(vmem_limit_bytes=VMEM_LIMIT),
        cost_estimate=pl.CostEstimate(flops=out_shape.size * 4, bytes_accessed=size, transcendentals=0),
    )(codes, *arrays)


def other_panels(packed):
    count = lax.axis_size("fsdp")
    if count == 2:
        return swapped(packed, "fsdp", 0)
    total = lax.psum(packed.astype(F32), "fsdp")
    return total - packed.astype(F32)


def shifted(block, axis, up, senders):
    step = 1 if up else -1
    return lax.ppermute(block, axis, [(dev, dev + step) for dev in senders])


def scatter_sum(parts):
    count = lax.axis_size("blk")
    me = lax.axis_index("blk")

    def term(owner):
        return lax.dynamic_index_in_dim(parts, jnp.clip(owner, 0, count - 1), 0, keepdims=False)

    total = term(me).astype(F32)
    for up in (True, False):
        held = None
        for step in range(1, count):
            owner = me + count - step if up else me - count + step
            block = term(owner)
            if held is not None:
                block = (block.astype(F32) + held.astype(F32)).astype(BF16)
            senders = range(0, step) if up else range(count - step, count)
            held = shifted(block, "blk", up, senders)
        if held is not None:
            total = total + held.astype(F32)
    return total


def gather_line(own):
    count = lax.axis_size("blk")
    me = lax.axis_index("blk")
    below, above = [], []
    for up, got in ((True, below), (False, above)):
        held = own
        for step in range(1, count):
            senders = range(step - 1, count - 1) if up else range(1, count - step + 1)
            held = shifted(held, "blk", up, senders)
            got.append(held)
    line = jnp.stack(below[::-1] + [own] + above)
    return lax.dynamic_slice_in_dim(line, count - 1 - me, count, 0)


def listed_tail(capacity, group_tokens, targets, enc_weight, enc_bias, dec_weight, present):
    tok_rows = targets.shape[0]
    latent_cols = enc_weight.shape[1]
    count = lax.axis_size("blk")
    data_count = lax.axis_size("dp")
    shard_index = lax.axis_index("blk")
    pair_index = lax.axis_index("dp")
    token_blocks = present.shape[0]
    grad_scale = 2.0 / token_blocks
    unit = int(np.gcd(tok_rows, TOKBLK))
    chunks = tok_rows // unit
    lat_blocks = latent_cols // LATBLK
    bias = enc_bias.reshape(1, latent_cols)
    by_dev = group_tokens.reshape(count, tok_rows, -1)
    rows = count * unit
    packed_shape = jax.ShapeDtypeStruct((capacity, unit, LATBLK), BF16)
    dense_shape = jax.ShapeDtypeStruct((rows, latent_cols), BF16)
    own_present = lax.dynamic_slice_in_dim(present, shard_index * lat_blocks, lat_blocks, 1)
    slots = jnp.arange(capacity, dtype=jnp.int32)

    def tiled(kernel):
        return functools.partial(kernel, lat_blocks, unit)

    codes, tokens_of, mine, other = [], [], [], []
    for chunk in range(chunks):
        first_row = (jnp.arange(count, dtype=jnp.int32) * data_count + pair_index) * tok_rows + chunk * unit
        onehot = (first_row // TOKBLK)[:, None] == jnp.arange(token_blocks, dtype=jnp.int32)[None, :]
        on = jnp.any(onehot[:, :, None] & own_present[None], axis=1).reshape(-1)
        index = jnp.arange(on.shape[0], dtype=jnp.int32)
        before = jnp.sum((on[None, :] & (index[None, :] < index[:, None])).astype(jnp.int32), axis=1)
        hit = on[None, :] & (before[None, :] == slots[:, None])
        code = jnp.sum(jnp.where(hit, index[None, :], 0), axis=1)
        codes.append(jnp.concatenate([code, jnp.sum(on.astype(jnp.int32))[None]]))
        tokens_of.append(by_dev[:, chunk * unit : (chunk + 1) * unit].reshape(rows, -1))
    for chunk in range(chunks):
        part = jnp.dot(tokens_of[chunk], enc_weight, preferred_element_type=F32).astype(BF16)
        mine.append(on_tiles(tiled(pack_kernel), packed_shape, codes[chunk], part))
        other.append(other_panels(mine[chunk]))
    acts, sums = [], []
    for chunk in range(chunks):
        acts.append(on_tiles(tiled(act_kernel), dense_shape, codes[chunk], mine[chunk], other[chunk], bias))
        part = jnp.einsum("tf,kfj->tkj", acts[chunk], dec_weight, preferred_element_type=F32).astype(BF16)
        sums.append(scatter_sum(part.reshape(count, unit, *part.shape[1:])))
    residuals, pre_grads = [], []
    for chunk in range(chunks):
        goal = targets[chunk * unit : (chunk + 1) * unit].astype(F32)
        own_grad = (grad_scale * (sums[chunk] - goal)).astype(BF16)
        line = gather_line(own_grad)
        residuals.append(line.reshape(rows, *line.shape[2:]))
    for chunk in range(chunks):
        back = jnp.einsum("tkj,kfj->tf", residuals[chunk], dec_weight, preferred_element_type=F32).astype(BF16)
        back_mine = on_tiles(tiled(pack_kernel), packed_shape, codes[chunk], back)
        back_other = other_panels(back_mine)
        pre_grads.append(
            on_tiles(
                tiled(pre_grad_kernel), dense_shape, codes[chunk], mine[chunk], other[chunk], bias,
                back_mine, back_other,
            )
        )
    return weight_grads(
        jnp.concatenate(tokens_of), jnp.concatenate(pre_grads), jnp.concatenate(acts), jnp.concatenate(residuals)
    )


def most_listed(present, tok_rows):
    count = lax.axis_size("blk")
    data_count = lax.axis_size("dp")
    unit = int(np.gcd(tok_rows, TOKBLK))
    chunks = tok_rows // unit
    per_shard = jnp.sum(present.reshape(present.shape[0], count, -1).astype(F32), axis=2)
    members = np.zeros((data_count * chunks, present.shape[0]), np.float32)
    for dev in range(count):
        for pair in range(data_count):
            for chunk in range(chunks):
                row = (dev * data_count + pair) * tok_rows + chunk * unit
                members[pair * chunks + chunk, row // TOKBLK] += 1.0
    return jnp.max(jnp.sum(members[:, :, None] * per_shard[None], axis=1)).astype(jnp.int32)


def on_device(tokens, targets, enc_weight, enc_bias, dec_weight, active_blocks):
    tok_rows = tokens.shape[0]
    lat_blocks = enc_weight.shape[1] // LATBLK
    all_blocks = lat_blocks * lax.axis_size("blk")
    present = jnp.any(
        active_blocks[:, :, None] == jnp.arange(all_blocks, dtype=jnp.int32)[None, None, :], axis=1
    )
    tiles = lax.axis_size("blk") * lat_blocks
    capacity = tiles * 7 // 16
    most = lax.pmax(most_listed(present, tok_rows), "parts")
    group_tokens = lax.all_gather(tokens, "blk", axis=0, tiled=True)
    return lax.cond(
        most <= capacity,
        lambda: listed_tail(capacity, group_tokens, targets, enc_weight, enc_bias, dec_weight, present),
        lambda: dense_tail(group_tokens, targets, enc_weight, enc_bias, dec_weight, active_blocks),
    )


def solution(mesh):
    return jax.shard_map(
        on_device,
        mesh=mesh,
        in_specs=(
            P(("parts", "blk", "dp"), "fsdp"),
            P(("parts", "blk", "dp"), None, "fsdp"),
            P("fsdp", "blk"),
            P("blk"),
            P(None, "blk", "fsdp"),
            P("parts", None),
        ),
        out_specs=(P(("parts", "fsdp", "dp"), "blk"), P("parts", "blk", ("fsdp", "dp"))),
        check_vma=False,
    )
```

time: 827 us -> 579 us (0.70); the launches traced: 825 us -> 568 us
  waiting for transfers between devices: 599 us -> 165 us
  starting transfers between devices: 0.4 us -> 92.4 us
  matrix products: 144 us -> 192 us
  Pallas kernels: 0 us -> 24.4 us
  other arithmetic: 43.1 us -> 29.3 us
  local copies, waits for them, and re-layouts: 24.5 us -> 34.4 us
  loops' own time: 0 us -> 9.38 us
    psum x2 -> x0, waiting for transfers between devices: 300 us -> none  [the longest x1 155 us: on_device(): lax.psum(back_part.astype(jnp.bfloat16), 'fsdp').astype(jnp.float32)]
    all_gather x1 -> x0, waiting for transfers between devices: 126 us -> none  [on_device(): residual_grad = lax.all_gather(own_grad, 'blk', axis=0, tiled=True)]
    reduce_scatter x1 -> x0, waiting for transfers between devices: 123 us -> none  [on_device(): lax.psum_scatter(jnp.einsum('tf,kfj->tkj', activations, dec_weight, prefe...]
    ppermute x0 -> x36, waiting for transfers between devices: none -> 117 us  [shifted(): return lax.ppermute(block, axis, [(dev, dev + step) for dev in senders])]
    ppermute x0 -> x36, starting transfers between devices: none -> 86.7 us  [shifted(): return lax.ppermute(block, axis, [(dev, dev + step) for dev in senders])]
    dot_general x6 -> x13, matrix products: 144 us -> 192 us  [the longest x3 55.9 us: listed_tail(): jnp.einsum('tkj,kfj->tf', residuals[chunk], dec_weight, preferred_element...]
    convert_element_type x4 -> x8, other arithmetic: 41.7 us -> 10.9 us  [the longest x6 7.35 us: scatter_sum(): block = (block.astype(F32) + held.astype(F32)).astype(BF16)]
    pallas_call x0 -> x12, Pallas kernels: none -> 24.4 us  [on_tiles(): pl.pallas_call(kernel, out_shape=out_shape, in_specs=[pl.BlockSpec(memory...]
  transfers between devices with their start and end apart: 7 -> 45, of which waited for: 6 -> 19; matrix products, arithmetic and copies ran while one was open for 9% -> 32% of each run, Pallas kernels for 0% -> 4%
where the time goes in v1:
time: 579 us; the launch traced here: 568 us
  matrix products  192 us (33%)
  waiting for transfers between devices  165 us (28%)
  starting transfers between devices  92.4 us (16%)
  local copies, waits for them, and re-layouts  34.4 us (6%)
  other arithmetic  29.3 us (5%)
  Pallas kernels  24.4 us (4%)
  between operations  15.9 us (3%)
  loops' own time  9.38 us (2%)
    ppermute x36, waiting for transfers between devices, shifted(): return lax.ppermute(block, axis, [(dev, dev + step) for dev in senders])  117 us
    ppermute x36, starting transfers between devices, shifted(): return lax.ppermute(block, axis, [(dev, dev + step) for dev in senders])  86.7 us
    dot_general x3, matrix products, listed_tail(): jnp.einsum('tkj,kfj->tf', residuals[chunk], dec_weight, preferred_element...  55.9 us
    dot_general x3, matrix products, listed_tail(): jnp.einsum('tf,kfj->tkj', acts[chunk], dec_weight, preferred_element_type...  53.8 us
    dot_general x2, matrix products, dec_of(): jnp.einsum('tf,tkj->kfj', activations, part, preferred_element_type=F32)  48.4 us
    all_gather x1, waiting for transfers between devices, on_device(): group_tokens = lax.all_gather(tokens, 'blk', axis=0, tiled=True)  31.9 us
    pallas_call x12, Pallas kernels, on_tiles(): pl.pallas_call(kernel, out_shape=out_shape, in_specs=[pl.BlockSpec(memory...  24.4 us
    unnamed x88, local copies, waits for them, and re-layouts  22.4 us
  transfers between devices with their start and end apart: 45, of which 19 were waited for; matrix products, arithmetic and copies ran while one was open for 32% of the time, Pallas kernels for 4%

profile of v1, /device:TPU:24, one launch (start us, length us, event | category | flops | bytes accessed | tf_op | source)
XLA Modules:
  0.0 568.0 jit_solution(5815750592863251182)
XLA Ops:
  17.1 31.9 %all-gather.5.cloned.1.call-done = bf16[768,1152]{1,0:T(8,128)(2,1)} async-done(((bf16[192,1152]{1,0:T(8,128)(2,1)}), bf16[768,1152]{1,0:T(8,128)(2,1)}) %all-gather.5.cloned.1.call-update) | async-done | bytes 1769488 | tf_op jit(solution)/shard_map/all_gather | solution.py:276
  49.0 511.5 %conditional.4 = (bf16[576,4096]{1,0:T(8,128)(2,1)}, bf16[4,4096,576]{1,2,0:T(8,128)(2,1)}) conditional(s32[]{:T(128)} %convert_element_type.379, (bf16[768,1152]{1,0:T(8,128)(2,1)}, s32[12,32]{1,0:T(8,128)}, bf16[1152,4096]{1,0:T(8,128)(2,1)}, f32[4096]{0:T(1024)}, bf16[4,4096,1152]{2,1,0:T(8,128)(2,1)}, ...), branch_computations={%region_5.10_spmd, %region_10.23_spmd} | conditional | flops 101709840384 | bytes 963619712
  61.3 6.8 %convolution_convert_fusion.8.dense_ref = bf16[256,4096]{1,0:T(8,128)(2,1)S(1)} fusion(bf16[256,1152]{1,0:T(8,128)(2,1)S(1)} %bitcast.225, bf16[1152,4096]{1,0:T(8,128)(2,1)} %get-tuple-element.44), kind=kOutput, calls=%fused_computation.73 | convolution fusion | flops 2416967680 | bytes 12124160 | tf_op jit(solution)/shard_map/cond/branch_1_fun/dot_general | solution.py:222
  71.9 6.8 %convolution_convert_fusion.7.dense_ref = bf16[256,4096]{1,0:T(8,128)(2,1)S(1)} fusion(bf16[256,1152]{1,0:T(8,128)(2,1)S(1)} %bitcast.229, bf16[1152,4096]{1,0:T(8,128)(2,1)} %get-tuple-element.44), kind=kOutput, calls=%fused_computation.72 | convolution fusion | flops 2416967680 | bytes 12124160 | tf_op jit(solution)/shard_map/cond/branch_1_fun/dot_general | solution.py:222
  82.8 6.8 %convolution_convert_fusion.6.dense_ref = bf16[256,4096]{1,0:T(8,128)(2,1)S(1)} fusion(bf16[256,1152]{1,0:T(8,128)(2,1)S(1)} %bitcast.227, bf16[1152,4096]{1,0:T(8,128)(2,1)} %get-tuple-element.44), kind=kOutput, calls=%fused_computation.71 | convolution fusion | flops 2416967680 | bytes 12124160 | tf_op jit(solution)/shard_map/cond/branch_1_fun/dot_general | solution.py:222
  94.8 17.9 %convolution_convert_fusion.11 = bf16[256,4,1152]{2,0,1:T(8,128)(2,1)} fusion(bf16[4,4096,1152]{2,1,0:T(8,128)(2,1)} %get-tuple-element.46, bf16[256,4096]{1,0:T(8,128)(2,1)S(1)} %branch_1_fun.13), kind=kOutput, calls=%fused_computation.78 | convolution fusion | flops 9664856064 | bytes 42205184 | tf_op jit(solution)/shard_map/cond/branch_1_fun/tf,kfj->tkj/dot_general | solution.py:228
  122.5 17.9 %convolution_convert_fusion.10 = bf16[256,4,1152]{2,0,1:T(8,128)(2,1)} fusion(bf16[4,4096,1152]{2,1,0:T(8,128)(2,1)} %get-tuple-element.46, bf16[256,4096]{1,0:T(8,128)(2,1)S(1)} %branch_1_fun.17), kind=kOutput, calls=%fused_computation.77 | convolution fusion | flops 9664856064 | bytes 42205184 | tf_op jit(solution)/shard_map/cond/branch_1_fun/tf,kfj->tkj/dot_general | solution.py:228
  147.5 18.0 %convolution_convert_fusion.9 = bf16[256,4,1152]{2,0,1:T(8,128)(2,1)} fusion(bf16[4,4096,1152]{2,1,0:T(8,128)(2,1)} %get-tuple-element.46, bf16[256,4096]{1,0:T(8,128)(2,1)S(1)} %branch_1_fun.21), kind=kOutput, calls=%fused_computation.76 | convolution fusion | flops 9664856064 | bytes 42205184 | tf_op jit(solution)/shard_map/cond/branch_1_fun/tf,kfj->tkj/dot_general | solution.py:228
  183.9 7.5 %collective-permute-start.35 = (bf16[64,4,1152]{2,0,1:T(8,128)(2,1)S(1)}, bf16[64,4,1152]{2,0,1:T(8,128)(2,1)S(1)}, u32[]{:S(2)}, u32[]{:S(2)}) collective-permute-start(bf16[64,4,1152]{2,0,1:T(8,128)(2,1)S(1)} %get-tuple-element.110), channel_id=1, source_target_pairs={{8,4},{12,8},{9,5},{13,9},{10,6},{14,10},{11,7},{15,11},{24,20},{2... | collective-permute-start | bytes 1769480 | tf_op jit(solution)/shard_map/cond/branch_1_fun/ppermute | solution.py:148
  197.9 7.5 %collective-permute-start.8 = (bf16[64,4,1152]{2,0,1:T(8,128)(2,1)}, bf16[64,4,1152]{2,0,1:T(8,128)(2,1)S(1)}, u32[]{:S(2)}, u32[]{:S(2)}) collective-permute-start(bf16[64,4,1152]{2,0,1:T(8,128)(2,1)} %get-tuple-element.96), channel_id=1, source_target_pairs={{4,0},{8,4},{12,8},{5,1},{9,5},{13,9},{6,2},{10,6},{14,10},{7,3},{... | collective-permute-start | bytes 1769480 | tf_op jit(solution)/shard_map/cond/branch_1_fun/ppermute | solution.py:148
  210.8 8.4 %collective-permute-start.22 = (bf16[64,4,1152]{2,0,1:T(8,128)(2,1)}, bf16[64,4,1152]{2,0,1:T(8,128)(2,1)}, u32[]{:S(2)}, u32[]{:S(2)}) collective-permute-start(bf16[64,4,1152]{2,0,1:T(8,128)(2,1)} %get-tuple-element.102), channel_id=1, source_target_pairs={{4,0},{8,4},{12,8},{5,1},{9,5},{13,9},{6,2},{10,6},{14,10},{7,3},{... | collective-permute-start | bytes 1769480 | tf_op jit(solution)/shard_map/cond/branch_1_fun/ppermute | solution.py:148
  223.4 8.4 %collective-permute-start.36 = (bf16[64,4,1152]{2,0,1:T(8,128)(2,1)}, bf16[64,4,1152]{2,0,1:T(8,128)(2,1)}, u32[]{:S(2)}, u32[]{:S(2)}) collective-permute-start(bf16[64,4,1152]{2,0,1:T(8,128)(2,1)} %get-tuple-element.108), channel_id=1, source_target_pairs={{4,0},{8,4},{12,8},{5,1},{9,5},{13,9},{6,2},{10,6},{14,10},{7,3},{... | collective-permute-start | bytes 1769480 | tf_op jit(solution)/shard_map/cond/branch_1_fun/ppermute | solution.py:148
  233.5 12.6 %collective-permute-done.22 = bf16[64,4,1152]{2,0,1:T(8,128)(2,1)} collective-permute-done((bf16[64,4,1152]{2,0,1:T(8,128)(2,1)}, bf16[64,4,1152]{2,0,1:T(8,128)(2,1)}, u32[]{:S(2)}, u32[]{:S(2)}) %collective-permute-start.22) | collective-permute-done | bytes 589856 | tf_op jit(solution)/shard_map/cond/branch_1_fun/ppermute | solution.py:148
  246.2 10.4 %collective-permute-done.36 = bf16[64,4,1152]{2,0,1:T(8,128)(2,1)} collective-permute-done((bf16[64,4,1152]{2,0,1:T(8,128)(2,1)}, bf16[64,4,1152]{2,0,1:T(8,128)(2,1)}, u32[]{:S(2)}, u32[]{:S(2)}) %collective-permute-start.36) | collective-permute-done | bytes 589856 | tf_op jit(solution)/shard_map/cond/branch_1_fun/ppermute | solution.py:148
  267.2 6.0 %collective-permute-start.26 = (bf16[64,4,1152]{2,0,1:T(8,128)(2,1)S(1)}, bf16[64,4,1152]{2,0,1:T(8,128)(2,1)}, u32[]{:S(2)}, u32[]{:S(2)}) collective-permute-start(bf16[64,4,1152]{2,0,1:T(8,128)(2,1)S(1)} %get-tuple-element.114), channel_id=1, source_target_pairs={{4,0},{8,4},{12,8},{5,1},{9,5},{13,9},{6,2},{10,6},{14,10},{7,3},{... | collective-permute-start | bytes 1769480 | tf_op jit(solution)/shard_map/cond/branch_1_fun/ppermute | solution.py:148
  278.3 5.2 collective-permute-start.40
  284.2 11.2 %collective-permute-done.37 = bf16[64,4,1152]{2,0,1:T(8,128)(2,1)S(1)} collective-permute-done((bf16[64,4,1152]{2,0,1:T(8,128)(2,1)S(1)}, bf16[64,4,1152]{2,0,1:T(8,128)(2,1)S(1)}, u32[]{:S(2)}, u32[]{:S(2)}) %collective-permute-start.37) | collective-permute-done | bytes 589856 | tf_op jit(solution)/shard_map/cond/branch_1_fun/ppermute | solution.py:148
  298.0 10.1 %collective-permute-done.23 = bf16[64,4,1152]{2,0,1:T(8,128)(2,1)} collective-permute-done((bf16[64,4,1152]{2,0,1:T(8,128)(2,1)S(1)}, bf16[64,4,1152]{2,0,1:T(8,128)(2,1)}, u32[]{:S(2)}, u32[]{:S(2)}) %collective-permute-start.23) | collective-permute-done | bytes 589856 | tf_op jit(solution)/shard_map/cond/branch_1_fun/ppermute | solution.py:148
  313.2 7.6 %collective-permute-done.38 = bf16[64,4,1152]{2,0,1:T(8,128)(2,1)} collective-permute-done((bf16[64,4,1152]{2,0,1:T(8,128)(2,1)S(1)}, bf16[64,4,1152]{2,0,1:T(8,128)(2,1)}, u32[]{:S(2)}, u32[]{:S(2)}) %collective-permute-start.38) | collective-permute-done | bytes 589856 | tf_op jit(solution)/shard_map/cond/branch_1_fun/ppermute | solution.py:148
  322.1 11.3 %collective-permute-done.10 = bf16[64,4,1152]{2,0,1:T(8,128)(2,1)} collective-permute-done((bf16[64,4,1152]{2,0,1:T(8,128)(2,1)}, bf16[64,4,1152]{2,0,1:T(8,128)(2,1)}, u32[]{:S(2)}, u32[]{:S(2)}) %collective-permute-start.10) | collective-permute-done | bytes 589856 | tf_op jit(solution)/shard_map/cond/branch_1_fun/ppermute | solution.py:148
  335.4 10.6 %collective-permute-done.24 = bf16[64,4,1152]{2,0,1:T(8,128)(2,1)} collective-permute-done((bf16[64,4,1152]{2,0,1:T(8,128)(2,1)}, bf16[64,4,1152]{2,0,1:T(8,128)(2,1)}, u32[]{:S(2)}, u32[]{:S(2)}) %collective-permute-start.24) | collective-permute-done | bytes 589856 | tf_op jit(solution)/shard_map/cond/branch_1_fun/ppermute | solution.py:148
  348.0 10.6 %collective-permute-done.39 = bf16[64,4,1152]{2,0,1:T(8,128)(2,1)} collective-permute-done((bf16[64,4,1152]{2,0,1:T(8,128)(2,1)}, bf16[64,4,1152]{2,0,1:T(8,128)(2,1)}, u32[]{:S(2)}, u32[]{:S(2)}) %collective-permute-start.39) | collective-permute-done | bytes 589856 | tf_op jit(solution)/shard_map/cond/branch_1_fun/ppermute | solution.py:148
  363.9 16.5 %collective-permute-done.25 = bf16[64,4,1152]{2,0,1:T(8,128)(2,1)S(1)} collective-permute-done((bf16[64,4,1152]{2,0,1:T(8,128)(2,1)}, bf16[64,4,1152]{2,0,1:T(8,128)(2,1)S(1)}, u32[]{:S(2)}, u32[]{:S(2)}) %collective-permute-start.25) | collective-permute-done | bytes 589856 | tf_op jit(solution)/shard_map/cond/branch_1_fun/ppermute | solution.py:148
  397.4 23.2 %convert_bitcast_fusion.1 = bf16[4,4096,576]{1,2,0:T(8,128)(2,1)} fusion(bf16[768,4,1152]{2,0,1:T(8,128)(2,1)} %pad_maximum_fusion, s32[]{:T(128)S(6)} %select_n.114, bf16[256,4096]{1,0:T(8,128)(2,1)} %copy-done.10, bf16[256,4096]{1,0:T(8,128)(2,1)} %copy-done.8, bf16[256,4096]{1,0:T(8,128)(2,1)} %copy-done.6), kind=kOutput, calls=%fused_computation.58 | convolution fusion | flops 14523826176 | bytes 29097988 | tf_op jit(solution)/shard_map/cond/branch_1_fun/tf,tkj->kfj/dot_general | solution.py:73
  420.5 18.6 %fusion.30.dense_ref = bf16[256,4096]{1,0:T(8,128)(2,1)} fusion(bf16[256,4,1152]{2,0,1:T(8,128)(2,1)} %bitcast.209, bf16[4,4096,1152]{2,1,0:T(8,128)(2,1)} %get-tuple-element.46), kind=kOutput, calls=%fused_computation.70 | convolution fusion | flops 9664724992 | bytes 42205184 | tf_op jit(solution)/shard_map/cond/branch_1_fun/tkj,kfj->tf/dot_general | solution.py:237
  443.2 18.7 %fusion.29.dense_ref = bf16[256,4096]{1,0:T(8,128)(2,1)} fusion(bf16[256,4,1152]{2,0,1:T(8,128)(2,1)} %bitcast.207, bf16[4,4096,1152]{2,1,0:T(8,128)(2,1)} %get-tuple-element.46), kind=kOutput, calls=%fused_computation.69 | convolution fusion | flops 9664724992 | bytes 42205184 | tf_op jit(solution)/shard_map/cond/branch_1_fun/tkj,kfj->tf/dot_general | solution.py:237
  468.0 18.5 %fusion.28.dense_ref = bf16[256,4096]{1,0:T(8,128)(2,1)} fusion(bf16[256,4,1152]{2,0,1:T(8,128)(2,1)} %bitcast.211, bf16[4,4096,1152]{2,1,0:T(8,128)(2,1)} %get-tuple-element.46), kind=kOutput, calls=%fused_computation.68 | convolution fusion | flops 9664724992 | bytes 42205184 | tf_op jit(solution)/shard_map/cond/branch_1_fun/tkj,kfj->tf/dot_general | solution.py:237
  497.2 14.6 %collective-permute-done.15.back_other_ref = bf16[56,64,128]{2,1,0:T(8,128)(2,1)S(1)} collective-permute-done((bf16[56,64,128]{2,1,0:T(8,128)(2,1)S(1)}, bf16[56,64,128]{2,1,0:T(8,128)(2,1)S(1)}, u32[]{:S(2)}, u32[]{:S(2)}) %collective-permute-start.15) | collective-permute-done | bytes 917536 | tf_op jit(solution)/shard_map/cond/branch_1_fun/ppermute | solution.py:25
  513.7 6.3 %convolution_convert_fusion.4 = bf16[576,4096]{1,0:T(8,128)(2,1)} fusion(bf16[256,4096]{1,0:T(8,128)(2,1)S(1)} %branch_1_fun.23, bf16[256,4096]{1,0:T(8,128)(2,1)S(1)} %branch_1_fun.19, bf16[256,4096]{1,0:T(8,128)(2,1)S(1)} %branch_1_fun.15, bf16[768,1152]{1,0:T(8,128)(2,1)S(1)} %pad_maximum_fusion.4, s32[]{:T(128)S(6)} %select_n.114), kind=kOutput, calls=%fused_computation.63 | convolution fusion | flops 3645112320 | bytes 11993092 | tf_op jit(solution)/shard_map/cond/branch_1_fun/ti,tf->if/dot_general | solution.py:77
  520.0 7.3 %convolution_convert_fusion.5 = bf16[576,4096]{1,0:T(8,128)(2,1)S(1)} fusion(bf16[256,4096]{1,0:T(8,128)(2,1)} %copy-done, bf16[256,4096]{1,0:T(8,128)(2,1)} %copy-done.1, bf16[256,4096]{1,0:T(8,128)(2,1)} %copy-done.2, bf16[768,1152]{1,0:T(8,128)(2,1)} %copy-done.29, s32[]{:T(128)S(6)} %select_n.105), kind=kOutput, calls=%fused_computation.64 | convolution fusion | flops 3645112320 | bytes 11993092 | tf_op jit(solution)/shard_map/cond/branch_1_fun/ti,tf->if/dot_general | solution.py:77
  528.2 6.8 %convert_add_fusion.1 = bf16[576,4096]{1,0:T(8,128)(2,1)} fusion(bf16[576,4096]{1,0:T(8,128)(2,1)} %collective-permute-done.44, bf16[576,4096]{1,0:T(8,128)(2,1)S(1)} %convolution_convert_fusion.5), kind=kLoop, calls=%fused_computation.59 | loop fusion | flops 9437184 | bytes 14155776 | tf_op jit(solution)/shard_map/cond/branch_1_fun/add | solution.py:83
  535.0 25.2 %bitcast_add_fusion.1 = bf16[4,4096,576]{1,2,0:T(8,128)(2,1)} fusion(bf16[4,4096,576]{1,2,0:T(8,128)(2,1)} %collective-permute-done.45, bf16[768,4,1152]{2,0,1:T(8,128)(2,1)} %pad_maximum_fusion, s32[]{:T(128)S(6)} %select_n.105, bf16[256,4096]{1,0:T(8,128)(2,1)S(1)} %copy-done.11, bf16[256,4096]{1,0:T(8,128)(2,1)S(1)} %copy-done.9, ...), kind=kOutput, calls=%fused_computation.57 | convolution fusion | flops 14561574912 | bytes 47972356 | tf_op jit(solution)/shard_map/cond/branch_1_fun/tf,tkj->kfj/dot_general | solution.py:73
  (227 shorter events, 153.4 us)
Async XLA Ops:
  7.2 41.8 %all-gather.5.cloned.1.call-start = ((), (), s32[]{:S(2)}) async-start(), calls=%async_computation.5 | async-start | bytes 2211840 | tf_op jit(solution)/shard_map/all_gather | solution.py:276
  81.0 39.7 %collective-permute-start.16 = (bf16[56,64,128]{2,1,0:T(8,128)(2,1)S(1)}, bf16[56,64,128]{2,1,0:T(8,128)(2,1)}, u32[]{:S(2)}, u32[]{:S(2)}) collective-permute-start(bf16[56,64,128]{2,1,0:T(8,128)(2,1)S(1)} %branch_1_fun.16.mine_ref), channel_id=1, source_target_pairs={{0,2},{2,0},{1,3},{3,1},{4,6},{6,4},{5,7},{7,5},{8,10},{10,8},{9,1... | collective-permute-start | bytes 2752520 | tf_op jit(solution)/shard_map/cond/branch_1_fun/ppermute | solution.py:25
  91.2 54.2 %collective-permute-start.30 = (bf16[56,64,128]{2,1,0:T(8,128)(2,1)S(1)}, bf16[56,64,128]{2,1,0:T(8,128)(2,1)}, u32[]{:S(2)}, u32[]{:S(2)}) collective-permute-start(bf16[56,64,128]{2,1,0:T(8,128)(2,1)S(1)} %branch_1_fun.20.mine_ref), channel_id=1, source_target_pairs={{0,2},{2,0},{1,3},{3,1},{4,6},{6,4},{5,7},{7,5},{8,10},{10,8},{9,1... | collective-permute-start | bytes 2752520 | tf_op jit(solution)/shard_map/cond/branch_1_fun/ppermute | solution.py:25
  115.1 52.7 %collective-permute-start.3 = (bf16[64,4,1152]{2,0,1:T(8,128)(2,1)}, bf16[64,4,1152]{2,0,1:T(8,128)(2,1)}, u32[]{:S(2)}, u32[]{:S(2)}) collective-permute-start(bf16[64,4,1152]{2,0,1:T(8,128)(2,1)} %get-tuple-element.99), channel_id=1, source_target_pairs={{0,4},{1,5},{2,6},{3,7},{16,20},{17,21},{18,22},{19,23}} | collective-permute-start | bytes 1769480 | tf_op jit(solution)/shard_map/cond/branch_1_fun/ppermute | solution.py:148
  116.6 52.5 %collective-permute-start.6 = (bf16[64,4,1152]{2,0,1:T(8,128)(2,1)}, bf16[64,4,1152]{2,0,1:T(8,128)(2,1)}, u32[]{:S(2)}, u32[]{:S(2)}) collective-permute-start(bf16[64,4,1152]{2,0,1:T(8,128)(2,1)} %get-tuple-element.100), channel_id=1, source_target_pairs={{12,8},{13,9},{14,10},{15,11},{28,24},{29,25},{30,26},{31,27}} | collective-permute-start | bytes 1769480 | tf_op jit(solution)/shard_map/cond/branch_1_fun/ppermute | solution.py:148
  142.6 29.4 %collective-permute-start.17 = (bf16[64,4,1152]{2,0,1:T(8,128)(2,1)}, bf16[64,4,1152]{2,0,1:T(8,128)(2,1)S(1)}, u32[]{:S(2)}, u32[]{:S(2)}) collective-permute-start(bf16[64,4,1152]{2,0,1:T(8,128)(2,1)} %get-tuple-element.105), channel_id=1, source_target_pairs={{0,4},{1,5},{2,6},{3,7},{16,20},{17,21},{18,22},{19,23}} | collective-permute-start | bytes 1769480 | tf_op jit(solution)/shard_map/cond/branch_1_fun/ppermute | solution.py:148
  143.3 30.0 %collective-permute-start.20 = (bf16[64,4,1152]{2,0,1:T(8,128)(2,1)S(1)}, bf16[64,4,1152]{2,0,1:T(8,128)(2,1)}, u32[]{:S(2)}, u32[]{:S(2)}) collective-permute-start(bf16[64,4,1152]{2,0,1:T(8,128)(2,1)S(1)} %get-tuple-element.106), channel_id=1, source_target_pairs={{12,8},{13,9},{14,10},{15,11},{28,24},{29,25},{30,26},{31,27}} | collective-permute-start | bytes 1769480 | tf_op jit(solution)/shard_map/cond/branch_1_fun/ppermute | solution.py:148
  175.4 32.8 %collective-permute-start.21 = (bf16[64,4,1152]{2,0,1:T(8,128)(2,1)S(1)}, bf16[64,4,1152]{2,0,1:T(8,128)(2,1)S(1)}, u32[]{:S(2)}, u32[]{:S(2)}) collective-permute-start(bf16[64,4,1152]{2,0,1:T(8,128)(2,1)S(1)} %get-tuple-element.104), channel_id=1, source_target_pairs={{8,4},{12,8},{9,5},{13,9},{10,6},{14,10},{11,7},{15,11},{24,20},{2... | collective-permute-start | bytes 1769480 | tf_op jit(solution)/shard_map/cond/branch_1_fun/ppermute | solution.py:148
  183.2 27.6 %collective-permute-start.32 = (bf16[64,4,1152]{2,0,1:T(8,128)(2,1)S(1)}, bf16[64,4,1152]{2,0,1:T(8,128)(2,1)S(1)}, u32[]{:S(2)}, u32[]{:S(2)}) collective-permute-start(bf16[64,4,1152]{2,0,1:T(8,128)(2,1)S(1)} %get-tuple-element.109), channel_id=1, source_target_pairs={{0,4},{4,8},{1,5},{5,9},{2,6},{6,10},{3,7},{7,11},{16,20},{20,24},... | collective-permute-start | bytes 1769480 | tf_op jit(solution)/shard_map/cond/branch_1_fun/ppermute | solution.py:148
  183.9 36.9 %collective-permute-start.35 = (bf16[64,4,1152]{2,0,1:T(8,128)(2,1)S(1)}, bf16[64,4,1152]{2,0,1:T(8,128)(2,1)S(1)}, u32[]{:S(2)}, u32[]{:S(2)}) collective-permute-start(bf16[64,4,1152]{2,0,1:T(8,128)(2,1)S(1)} %get-tuple-element.110), channel_id=1, source_target_pairs={{8,4},{12,8},{9,5},{13,9},{10,6},{14,10},{11,7},{15,11},{24,20},{2... | collective-permute-start | bytes 1769480 | tf_op jit(solution)/shard_map/cond/branch_1_fun/ppermute | solution.py:148
  196.6 26.8 %collective-permute-start.5 = (bf16[64,4,1152]{2,0,1:T(8,128)(2,1)S(1)}, bf16[64,4,1152]{2,0,1:T(8,128)(2,1)}, u32[]{:S(2)}, u32[]{:S(2)}) collective-permute-start(bf16[64,4,1152]{2,0,1:T(8,128)(2,1)S(1)} %get-tuple-element.95), channel_id=1, source_target_pairs={{0,4},{4,8},{8,12},{1,5},{5,9},{9,13},{2,6},{6,10},{10,14},{3,7},{... | collective-permute-start | bytes 1769480 | tf_op jit(solution)/shard_map/cond/branch_1_fun/ppermute | solution.py:148
  197.9 35.6 %collective-permute-start.8 = (bf16[64,4,1152]{2,0,1:T(8,128)(2,1)}, bf16[64,4,1152]{2,0,1:T(8,128)(2,1)S(1)}, u32[]{:S(2)}, u32[]{:S(2)}) collective-permute-start(bf16[64,4,1152]{2,0,1:T(8,128)(2,1)} %get-tuple-element.96), channel_id=1, source_target_pairs={{4,0},{8,4},{12,8},{5,1},{9,5},{13,9},{6,2},{10,6},{14,10},{7,3},{... | collective-permute-start | bytes 1769480 | tf_op jit(solution)/shard_map/cond/branch_1_fun/ppermute | solution.py:148
  210.8 35.4 %collective-permute-start.22 = (bf16[64,4,1152]{2,0,1:T(8,128)(2,1)}, bf16[64,4,1152]{2,0,1:T(8,128)(2,1)}, u32[]{:S(2)}, u32[]{:S(2)}) collective-permute-start(bf16[64,4,1152]{2,0,1:T(8,128)(2,1)} %get-tuple-element.102), channel_id=1, source_target_pairs={{4,0},{8,4},{12,8},{5,1},{9,5},{13,9},{6,2},{10,6},{14,10},{7,3},{... | collective-permute-start | bytes 1769480 | tf_op jit(solution)/shard_map/cond/branch_1_fun/ppermute | solution.py:148
  223.4 33.1 %collective-permute-start.36 = (bf16[64,4,1152]{2,0,1:T(8,128)(2,1)}, bf16[64,4,1152]{2,0,1:T(8,128)(2,1)}, u32[]{:S(2)}, u32[]{:S(2)}) collective-permute-start(bf16[64,4,1152]{2,0,1:T(8,128)(2,1)} %get-tuple-element.108), channel_id=1, source_target_pairs={{4,0},{8,4},{12,8},{5,1},{9,5},{13,9},{6,2},{10,6},{14,10},{7,3},{... | collective-permute-start | bytes 1769480 | tf_op jit(solution)/shard_map/cond/branch_1_fun/ppermute | solution.py:148
  265.9 29.5 %collective-permute-start.37 = (bf16[64,4,1152]{2,0,1:T(8,128)(2,1)S(1)}, bf16[64,4,1152]{2,0,1:T(8,128)(2,1)S(1)}, u32[]{:S(2)}, u32[]{:S(2)}) collective-permute-start(bf16[64,4,1152]{2,0,1:T(8,128)(2,1)S(1)} %get-tuple-element.115), channel_id=1, source_target_pairs={{0,4},{4,8},{8,12},{1,5},{5,9},{9,13},{2,6},{6,10},{10,14},{3,7},{... | collective-permute-start | bytes 1769480 | tf_op jit(solution)/shard_map/cond/branch_1_fun/ppermute | solution.py:148
  267.2 29.5 %collective-permute-start.26 = (bf16[64,4,1152]{2,0,1:T(8,128)(2,1)S(1)}, bf16[64,4,1152]{2,0,1:T(8,128)(2,1)}, u32[]{:S(2)}, u32[]{:S(2)}) collective-permute-start(bf16[64,4,1152]{2,0,1:T(8,128)(2,1)S(1)} %get-tuple-element.114), channel_id=1, source_target_pairs={{4,0},{8,4},{12,8},{5,1},{9,5},{13,9},{6,2},{10,6},{14,10},{7,3},{... | collective-permute-start | bytes 1769480 | tf_op jit(solution)/shard_map/cond/branch_1_fun/ppermute | solution.py:148
  273.2 34.9 %collective-permute-start.23 = (bf16[64,4,1152]{2,0,1:T(8,128)(2,1)S(1)}, bf16[64,4,1152]{2,0,1:T(8,128)(2,1)}, u32[]{:S(2)}, u32[]{:S(2)}) collective-permute-start(bf16[64,4,1152]{2,0,1:T(8,128)(2,1)S(1)} %get-tuple-element.114), channel_id=1, source_target_pairs={{0,4},{4,8},{8,12},{1,5},{5,9},{9,13},{2,6},{6,10},{10,14},{3,7},{... | collective-permute-start | bytes 1769480 | tf_op jit(solution)/shard_map/cond/branch_1_fun/ppermute | solution.py:148
  278.3 31.3 %collective-permute-start.40 = (bf16[64,4,1152]{2,0,1:T(8,128)(2,1)S(1)}, bf16[64,4,1152]{2,0,1:T(8,128)(2,1)}, u32[]{:S(2)}, u32[]{:S(2)}) collective-permute-start(bf16[64,4,1152]{2,0,1:T(8,128)(2,1)S(1)} %get-tuple-element.115), channel_id=1, source_target_pairs={{4,0},{8,4},{12,8},{5,1},{9,5},{13,9},{6,2},{10,6},{14,10},{7,3},{... | collective-permute-start | bytes 1769480 | tf_op jit(solution)/shard_map/cond/branch_1_fun/ppermute | solution.py:148
  283.5 27.4 %collective-permute-start.13 = (bf16[64,4,1152]{2,0,1:T(8,128)(2,1)S(1)}, bf16[64,4,1152]{2,0,1:T(8,128)(2,1)S(1)}, u32[]{:S(2)}, u32[]{:S(2)}) collective-permute-start(bf16[64,4,1152]{2,0,1:T(8,128)(2,1)S(1)} %collective-permute-done.12), channel_id=1, source_target_pairs={{4,0},{8,4},{5,1},{9,5},{6,2},{10,6},{7,3},{11,7},{20,16},{24,20},... | collective-permute-start | bytes 1769480 | tf_op jit(solution)/shard_map/cond/branch_1_fun/ppermute | solution.py:148
  296.7 36.7 %collective-permute-start.10 = (bf16[64,4,1152]{2,0,1:T(8,128)(2,1)}, bf16[64,4,1152]{2,0,1:T(8,128)(2,1)}, u32[]{:S(2)}, u32[]{:S(2)}) collective-permute-start(bf16[64,4,1152]{2,0,1:T(8,128)(2,1)} %collective-permute-done.9), channel_id=1, source_target_pairs={{4,8},{8,12},{5,9},{9,13},{6,10},{10,14},{7,11},{11,15},{20,24},{2... | collective-permute-start | bytes 1769480 | tf_op jit(solution)/shard_map/cond/branch_1_fun/ppermute | solution.py:148
  308.1 26.0 %collective-permute-start.27 = (bf16[64,4,1152]{2,0,1:T(8,128)(2,1)}, bf16[64,4,1152]{2,0,1:T(8,128)(2,1)}, u32[]{:S(2)}, u32[]{:S(2)}) collective-permute-start(bf16[64,4,1152]{2,0,1:T(8,128)(2,1)} %collective-permute-done.26), channel_id=1, source_target_pairs={{4,0},{8,4},{5,1},{9,5},{6,2},{10,6},{7,3},{11,7},{20,16},{24,20},... | collective-permute-start | bytes 1769480 | tf_op jit(solution)/shard_map/cond/branch_1_fun/ppermute | solution.py:148
  309.6 36.4 %collective-permute-start.24 = (bf16[64,4,1152]{2,0,1:T(8,128)(2,1)}, bf16[64,4,1152]{2,0,1:T(8,128)(2,1)}, u32[]{:S(2)}, u32[]{:S(2)}) collective-permute-start(bf16[64,4,1152]{2,0,1:T(8,128)(2,1)} %collective-permute-done.23), channel_id=1, source_target_pairs={{4,8},{8,12},{5,9},{9,13},{6,10},{10,14},{7,11},{11,15},{20,24},{2... | collective-permute-start | bytes 1769480 | tf_op jit(solution)/shard_map/cond/branch_1_fun/ppermute | solution.py:148
  311.7 35.0 %collective-permute-start.41 = (bf16[64,4,1152]{2,0,1:T(8,128)(2,1)}, bf16[64,4,1152]{2,0,1:T(8,128)(2,1)}, u32[]{:S(2)}, u32[]{:S(2)}) collective-permute-start(bf16[64,4,1152]{2,0,1:T(8,128)(2,1)} %collective-permute-done.40), channel_id=1, source_target_pairs={{4,0},{8,4},{5,1},{9,5},{6,2},{10,6},{7,3},{11,7},{20,16},{24,20},... | collective-permute-start | bytes 1769480 | tf_op jit(solution)/shard_map/cond/branch_1_fun/ppermute | solution.py:148
  320.7 37.9 %collective-permute-start.39 = (bf16[64,4,1152]{2,0,1:T(8,128)(2,1)}, bf16[64,4,1152]{2,0,1:T(8,128)(2,1)}, u32[]{:S(2)}, u32[]{:S(2)}) collective-permute-start(bf16[64,4,1152]{2,0,1:T(8,128)(2,1)} %collective-permute-done.38), channel_id=1, source_target_pairs={{8,12},{9,13},{10,14},{11,15},{24,28},{25,29},{26,30},{27,31}} | collective-permute-start | bytes 1769480 | tf_op jit(solution)/shard_map/cond/branch_1_fun/ppermute | solution.py:148
  333.4 58.4 %collective-permute-start.14 = (bf16[64,4,1152]{2,0,1:T(8,128)(2,1)}, bf16[64,4,1152]{2,0,1:T(8,128)(2,1)S(1)}, u32[]{:S(2)}, u32[]{:S(2)}) collective-permute-start(bf16[64,4,1152]{2,0,1:T(8,128)(2,1)} %copy-done.36), channel_id=1, source_target_pairs={{4,0},{5,1},{6,2},{7,3},{20,16},{21,17},{22,18},{23,19}} | collective-permute-start | bytes 1769480 | tf_op jit(solution)/shard_map/cond/branch_1_fun/ppermute | solution.py:148
  334.1 48.7 %collective-permute-start.11 = (bf16[64,4,1152]{2,0,1:T(8,128)(2,1)}, bf16[64,4,1152]{2,0,1:T(8,128)(2,1)S(1)}, u32[]{:S(2)}, u32[]{:S(2)}) collective-permute-start(bf16[64,4,1152]{2,0,1:T(8,128)(2,1)} %collective-permute-done.10), channel_id=1, source_target_pairs={{8,12},{9,13},{10,14},{11,15},{24,28},{25,29},{26,30},{27,31}} | collective-permute-start | bytes 1769480 | tf_op jit(solution)/shard_map/cond/branch_1_fun/ppermute | solution.py:148
  346.0 44.2 %collective-permute-start.28 = (bf16[64,4,1152]{2,0,1:T(8,128)(2,1)}, bf16[64,4,1152]{2,0,1:T(8,128)(2,1)S(1)}, u32[]{:S(2)}, u32[]{:S(2)}) collective-permute-start(bf16[64,4,1152]{2,0,1:T(8,128)(2,1)} %collective-permute-done.27), channel_id=1, source_target_pairs={{4,0},{5,1},{6,2},{7,3},{20,16},{21,17},{22,18},{23,19}} | collective-permute-start | bytes 1769480 | tf_op jit(solution)/shard_map/cond/branch_1_fun/ppermute | solution.py:148
  346.7 33.6 %collective-permute-start.25 = (bf16[64,4,1152]{2,0,1:T(8,128)(2,1)}, bf16[64,4,1152]{2,0,1:T(8,128)(2,1)S(1)}, u32[]{:S(2)}, u32[]{:S(2)}) collective-permute-start(bf16[64,4,1152]{2,0,1:T(8,128)(2,1)} %collective-permute-done.24), channel_id=1, source_target_pairs={{8,12},{9,13},{10,14},{11,15},{24,28},{25,29},{26,30},{27,31}} | collective-permute-start | bytes 1769480 | tf_op jit(solution)/shard_map/cond/branch_1_fun/ppermute | solution.py:148
  358.7 31.2 %collective-permute-start.42 = (bf16[64,4,1152]{2,0,1:T(8,128)(2,1)}, bf16[64,4,1152]{2,0,1:T(8,128)(2,1)S(1)}, u32[]{:S(2)}, u32[]{:S(2)}) collective-permute-start(bf16[64,4,1152]{2,0,1:T(8,128)(2,1)} %collective-permute-done.41), channel_id=1, source_target_pairs={{4,0},{5,1},{6,2},{7,3},{20,16},{21,17},{22,18},{23,19}} | collective-permute-start | bytes 1769480 | tf_op jit(solution)/shard_map/cond/branch_1_fun/ppermute | solution.py:148
  420.5 114.5 %collective-permute-start.45 = (bf16[4,4096,576]{1,2,0:T(8,128)(2,1)}, bf16[4,4096,576]{1,2,0:T(8,128)(2,1)}, u32[]{:S(2)}, u32[]{:S(2)}) collective-permute-start(bf16[4,4096,576]{1,2,0:T(8,128)(2,1)} %convert_bitcast_fusion.1), channel_id=1, source_target_pairs={{0,1},{1,0},{2,3},{3,2},{4,5},{5,4},{6,7},{7,6},{8,9},{9,8},{10,11... | collective-permute-start | bytes 56623112 | tf_op jit(solution)/shard_map/cond/branch_1_fun/ppermute | solution.py:25
  443.2 48.0 %collective-permute-start.43 = (bf16[56,64,128]{2,1,0:T(8,128)(2,1)}, bf16[56,64,128]{2,1,0:T(8,128)(2,1)}, u32[]{:S(2)}, u32[]{:S(2)}) collective-permute-start(bf16[56,64,128]{2,1,0:T(8,128)(2,1)} %branch_1_fun.22.back_mine_ref), channel_id=1, source_target_pairs={{0,2},{2,0},{1,3},{3,1},{4,6},{6,4},{5,7},{7,5},{8,10},{10,8},{9,1... | collective-permute-start | bytes 2752520 | tf_op jit(solution)/shard_map/cond/branch_1_fun/ppermute | solution.py:25
  465.9 28.2 %collective-permute-start.29 = (bf16[56,64,128]{2,1,0:T(8,128)(2,1)}, bf16[56,64,128]{2,1,0:T(8,128)(2,1)}, u32[]{:S(2)}, u32[]{:S(2)}) collective-permute-start(bf16[56,64,128]{2,1,0:T(8,128)(2,1)} %branch_1_fun.18.back_mine_ref), channel_id=1, source_target_pairs={{0,2},{2,0},{1,3},{3,1},{4,6},{6,4},{5,7},{7,5},{8,10},{10,8},{9,1... | collective-permute-start | bytes 2752520 | tf_op jit(solution)/shard_map/cond/branch_1_fun/ppermute | solution.py:25
  (48 other events, 723.7 us)
Sparse Core Ops, SparseCore 0:
  9.6 39.3 all-gather.4
